TPU v7x, 32 devices: a whole 2x2x4 slice. The times are simulated.
32 devices in a mesh: row: 8 (over z, y), col: 4 (over x, core).
Axes of the slice: x: 2, y: 2, z: 4, core: 2. Of those that a mesh axis runs over, the one named last changes fastest.
Arguments:
- blocks: bfloat16 [16384, 128, 128], P(('row', 'col')), may hold values from -0.046875 to 0.046875
- coords: int32 [16384, 2], P(('row', 'col')), may hold values from 0 to 31, as said below
- counts: int32 [32], P(('row', 'col')), may hold values from 1 to 512, as said below
- start_block: float32 [16384, 64], P(('row', 'col')), may hold values from -12 to 12, as said below
Outputs:
- lanczos_basis: float32 [16384, 64], P(('row', 'col'))
- diag_blocks: float32 [2, 64, 64], replicated
- upper_blocks: float32 [2, 64, 64], replicated
Inputs may be any that keep to these rules, and one draw needn't show every extreme that they name: `coords`: within one device's 512 slots the coordinate pairs are distinct; block rows lie below 16 and block columns below 32. `counts`: slot s of a device is live exactly when s is below the device's count; some device has all 512 slots live in every draw. `start_block`: finite values of order one.
All inputs are finite; a program needn't handle non-finite values.
Results may differ from a plain program's by a relative error of at most 0.0049.
Values may be sent and summed in bfloat16 or wider, within the bound.
A program may use at most 128 MiB of HBM per device.

v0:
```python
import jax
import jax.numpy as jnp
from jax import lax
from jax.sharding import PartitionSpec as P

ITERS = 2


def orthonormal(panel, gram_now):
    lower = jnp.linalg.cholesky(gram_now)
    inverse = jax.scipy.linalg.solve_triangular(
        lower, jnp.eye(gram_now.shape[0], dtype=jnp.float32), lower=True
    )
    return (jnp.dot(panel, inverse.T, precision=lax.Precision.HIGHEST), lower.T)


def local_product(blocks, coords, live_count, row_x, col_x):
    slot_total = blocks.shape[0]
    group_size = min(128, slot_total)
    row_blocks = row_x.shape[0]
    col_blocks = col_x.shape[0]
    tile_rows = row_x.shape[1]
    vec_width = row_x.shape[2]
    turn_count = (live_count + group_size - 1) // group_size
    row_ids = jnp.arange(row_blocks, dtype=jnp.int32)

    def one_turn(turn, carry):
        row_total, col_total = carry
        first_slot = turn * group_size
        slab = lax.dynamic_slice_in_dim(blocks, first_slot, group_size, 0)
        pairs = lax.dynamic_slice_in_dim(coords, first_slot, group_size, 0)
        live_mask = (first_slot + jnp.arange(group_size, dtype=jnp.int32) < live_count).astype(
            jnp.float32
        )
        row_index = pairs[:, 0]
        col_index = pairs[:, 1]
        col_rows = jnp.take(col_x, col_index, axis=0)
        forward = jnp.einsum("gij,gjk->gik", slab, col_rows, preferred_element_type=jnp.float32)
        row_onehot = (row_index[:, None] == row_ids[None, :]).astype(jnp.float32) * live_mask[
            :, None
        ]
        row_total = row_total + jnp.einsum(
            "gr,gik->rik", row_onehot, forward, precision=lax.Precision.HIGHEST
        )
        row_rows = jnp.take(row_x, row_index, axis=0)
        backward = jnp.einsum("gij,gik->gjk", slab, row_rows, preferred_element_type=jnp.float32)
        col_total = col_total + jax.ops.segment_sum(
            backward * live_mask[:, None, None], col_index, num_segments=col_blocks
        )
        return (row_total, col_total)

    start_rows = jnp.zeros((row_blocks, tile_rows, vec_width), jnp.float32)
    start_cols = jnp.zeros((col_blocks, tile_rows, vec_width), jnp.float32)
    return lax.fori_loop(0, turn_count, one_turn, (start_rows, start_cols))


def redistribute(packed, tile_rows):
    rows_dev, vec_width = packed.shape
    n_row = lax.axis_size("row")
    n_col = lax.axis_size("col")
    gathered = lax.all_gather(packed, ("row", "col"), axis=0, tiled=True)
    row_start = lax.axis_index("row") * (n_col * rows_dev)
    row_part = lax.dynamic_slice_in_dim(gathered, row_start, n_col * rows_dev, 0)
    grid_view = gathered.reshape(n_row, n_col, rows_dev, vec_width)
    col_part = lax.dynamic_index_in_dim(grid_view, lax.axis_index("col"), 1, keepdims=False)
    row_x = row_part.reshape(-1, tile_rows, vec_width)
    col_x = col_part.reshape(-1, tile_rows, vec_width)
    return (row_x, col_x)


def per_device(blocks, coords, counts, start_block):
    high = lax.Precision.HIGHEST
    rows_dev, vec_width = start_block.shape
    tile_rows = blocks.shape[1]
    row_total = float(rows_dev * lax.axis_size("row") * lax.axis_size("col"))
    first_gram = (
        lax.psum(jnp.dot(start_block.T, start_block, precision=high), ("row", "col")) / row_total
    )
    current, unused = orthonormal(start_block, first_gram)
    previous = jnp.zeros_like(current)
    diagonal_list = []
    upper_list = []
    for iteration in range(ITERS):
        packed = current.astype(jnp.bfloat16)
        row_x, col_x = redistribute(packed, tile_rows)
        part_rows, part_cols = local_product(blocks, coords, counts[0], row_x, col_x)
        summed_rows = lax.psum_scatter(
            part_rows.reshape(-1, vec_width), "col", scatter_dimension=0, tiled=True
        )
        summed_cols = lax.psum_scatter(
            part_cols.reshape(-1, vec_width), "row", scatter_dimension=0, tiled=True
        )
        applied = current + summed_rows + summed_cols
        proj_part, back_part = lax.psum(
            (
                jnp.dot(current.T, applied, precision=high),
                jnp.dot(previous.T, applied, precision=high),
            ),
            ("row", "col"),
        )
        along_now = proj_part / row_total
        along_prev = back_part / row_total
        residual = (
            applied
            - jnp.dot(current, along_now, precision=high)
            - jnp.dot(previous, along_prev, precision=high)
        )
        resid_gram = (
            lax.psum(jnp.dot(residual.T, residual, precision=high), ("row", "col")) / row_total
        )
        next_basis, upper = orthonormal(residual, resid_gram)
        diagonal_list.append(along_now)
        upper_list.append(upper)
        previous, current = (current, next_basis)
    return (current, jnp.stack(diagonal_list), jnp.stack(upper_list))


def solution(mesh):
    return jax.shard_map(
        per_device,
        mesh=mesh,
        in_specs=(
            P(("row", "col"), None, None),
            P(("row", "col"), None),
            P(("row", "col")),
            P(("row", "col"), None),
        ),
        out_specs=(P(("row", "col"), None), P(), P()),
        check_vma=False,
    )
```

profile of v0, /device:TPU:0, one launch (start us, length us, event | category | flops | bytes accessed | tf_op | source)
XLA Modules:
  0.0 877.2 jit_solution(17112685095898486763)
XLA Ops:
  8.3 42.2 %psum.49 = f32[64,64]{0,1:T(8,128)S(1)} all-reduce(f32[64,64]{0,1:T(8,128)S(1)} %fusion.97), channel_id=1, replica_groups=mesh['row'=8,'col'=4] {'row','col'}, use_global_device_ids=true, to_apply=%region_0.0 | all-reduce | flops 4096 | bytes 32768 | tf_op jit(solution)/shard_map/psum | solution.py:77
  50.6 5.8 cholesky.59
  57.8 4.9 custom-call.7
  64.6 54.3 %all-gather.3.cloned.1.call-done = bf16[16384,64]{0,1:T(8,128)(2,1)} async-done(((bf16[512,64]{0,1:T(8,128)(2,1)}), bf16[16384,64]{0,1:T(8,128)(2,1)}) %all-gather.3.cloned.1.call-update) | async-done | bytes 2097168 | tf_op jit(solution)/shard_map/all_gather | solution.py:61
  126.0 38.5 %while.26 = (s32[]{:T(128)}, f32[16,128,64]{1,0,2:T(8,128)S(1)}, f32[32,128,64]{1,2,0:T(8,128)S(1)}, s32[]{:T(128)}, s32[512,2]{0,1:T(2,128)S(1)}, /*index=5*/s3...) while((s32[]{:T(128)}, f32[16,128,64]{1,0,2:T(8,128)S(1)}, ...), condition=%wide.region_5.10_spmd.clone, body=%wide.region_3.9_spmd.clone.sunk | while | flops 742530944 | bytes 51399880 | solution.py:54
  129.2 6.6 fusion.143
  143.9 7.0 broadcast_multiply_fusion.7
  150.9 13.5 %scatter_fusion = f32[32,128,64]{1,2,0:T(8,128)S(1)} fusion(f32[32,128,64]{1,2,0:T(8,128)S(1)} %get-tuple-element.412, s32[128]{0:T(128)S(1)} %get-tuple-element.377, f32[128,128,64]{1,2,0:T(8,128)} %broadcast_multiply_fusion.7), kind=kCustom, calls=%fused_computation.4.clone.clone.1 | custom fusion | flops 1048576 | bytes 12583424 | tf_op jit(solution)/shard_map/while/body/scatter-add | solution.py:47
  166.6 134.5 %reduce-scatter.5.cloned.1.call-done = f32[512,64]{0,1:T(8,128)} async-done(((f32[2048,64]{0,1:T(8,128)}), f32[512,64]{0,1:T(8,128)}) %reduce-scatter.5.cloned.1.call-update) | async-done | bytes 131088 | tf_op jit(solution)/shard_map/reduce_scatter | solution.py:87
  301.1 67.3 %reduce-scatter.7.cloned.1.call-done = f32[512,64]{0,1:T(8,128)} async-done(((f32[4096,64]{0,1:T(8,128)}), f32[512,64]{0,1:T(8,128)}) %reduce-scatter.7.cloned.1.call-update) | async-done | bytes 131088 | tf_op jit(solution)/shard_map/reduce_scatter | solution.py:90
  370.8 40.7 %all-reduce.1 = (f32[64,64]{0,1:T(8,128)S(1)}, f32[64,64]{0,1:T(8,128)S(1)}) all-reduce(f32[64,64]{0,1:T(8,128)S(1)} %fusion.64, f32[64,64]{0,1:T(8,128)S(1)} %fusion.94), channel_id=1, replica_groups=mesh['row'=8,'col'=4] {'row','col'}, use_global_device_ids=true, to_apply=%region_9.14 | all-reduce | flops 8192 | bytes 65536 | tf_op jit(solution)/shard_map/psum | solution.py:94
  413.1 39.4 %psum.52 = f32[64,64]{0,1:T(8,128)S(1)} all-reduce(f32[64,64]{0,1:T(8,128)S(1)} %fusion.98), channel_id=1, replica_groups=mesh['row'=8,'col'=4] {'row','col'}, use_global_device_ids=true, to_apply=%region_11.16 | all-reduce | flops 4096 | bytes 32768 | tf_op jit(solution)/shard_map/psum | solution.py:109
  452.6 5.8 cholesky.70
  466.5 54.9 %all-gather.5.cloned.1.call-done = bf16[16384,64]{0,1:T(8,128)(2,1)} async-done(((bf16[512,64]{0,1:T(8,128)(2,1)}), bf16[16384,64]{0,1:T(8,128)(2,1)}) %all-gather.5.cloned.1.call-update) | async-done | bytes 2097168 | tf_op jit(solution)/shard_map/all_gather | solution.py:61
  528.6 38.3 %while.27 = (s32[]{:T(128)}, f32[16,128,64]{1,0,2:T(8,128)S(1)}, f32[32,128,64]{1,2,0:T(8,128)S(1)}, s32[]{:T(128)}, s32[512,2]{0,1:T(2,128)S(1)}, /*index=5*/s3...) while((s32[]{:T(128)}, f32[16,128,64]{1,0,2:T(8,128)S(1)}, ...), condition=%wide.region_14.19_spmd.clone, body=%wide.region_12.18_spmd.clone.sunk | while | flops 742530944 | bytes 51399880 | solution.py:54
  531.6 6.6 fusion.151
  546.3 7.0 broadcast_multiply_fusion.8
  553.4 13.5 %scatter_fusion.1 = f32[32,128,64]{1,2,0:T(8,128)S(1)} fusion(f32[32,128,64]{1,2,0:T(8,128)S(1)} %get-tuple-element.451, s32[128]{0:T(128)S(1)} %get-tuple-element.394, f32[128,128,64]{1,2,0:T(8,128)} %broadcast_multiply_fusion.8), kind=kCustom, calls=%fused_computation.5.clone.clone.1 | custom fusion | flops 1048576 | bytes 12583424 | tf_op jit(solution)/shard_map/while/body/scatter-add | solution.py:47
  569.1 134.5 %reduce-scatter.9.cloned.1.call-done = f32[512,64]{0,1:T(8,128)} async-done(((f32[2048,64]{0,1:T(8,128)}), f32[512,64]{0,1:T(8,128)}) %reduce-scatter.9.cloned.1.call-update) | async-done | bytes 131088 | tf_op jit(solution)/shard_map/reduce_scatter | solution.py:87
  703.6 67.2 %reduce-scatter.11.cloned.1.call-done = f32[512,64]{0,1:T(8,128)} async-done(((f32[4096,64]{0,1:T(8,128)}), f32[512,64]{0,1:T(8,128)}) %reduce-scatter.11.cloned.1.call-update) | async-done | bytes 131088 | tf_op jit(solution)/shard_map/reduce_scatter | solution.py:90
  773.2 40.8 %all-reduce = (f32[64,64]{0,1:T(8,128)S(1)}, f32[64,64]{0,1:T(8,128)S(1)}) all-reduce(f32[64,64]{0,1:T(8,128)S(1)} %fusion.92, f32[64,64]{0,1:T(8,128)S(1)} %fusion.91), channel_id=1, replica_groups=mesh['row'=8,'col'=4] {'row','col'}, use_global_device_ids=true, to_apply=%region_17.22 | all-reduce | flops 8192 | bytes 65536 | tf_op jit(solution)/shard_map/psum | solution.py:94
  815.8 39.3 %psum.55 = f32[64,64]{0,1:T(8,128)S(1)} all-reduce(f32[64,64]{0,1:T(8,128)S(1)} %fusion.99), channel_id=1, replica_groups=mesh['row'=8,'col'=4] {'row','col'}, use_global_device_ids=true, to_apply=%region_19.24 | all-reduce | flops 4096 | bytes 32768 | tf_op jit(solution)/shard_map/psum | solution.py:109
  855.2 5.8 cholesky.81
  862.4 4.9 custom-call.9
  (100 shorter events, 64.7 us)
Async XLA Ops:
  7.2 0.9 copy-start
  7.2 111.7 %all-gather.3.cloned.1.call-start = ((), (), s32[]{:S(2)}) async-start(), calls=%async_computation.4 | async-start | bytes 2162688 | tf_op jit(solution)/shard_map/all_gather | solution.py:61
  63.9 237.2 %reduce-scatter.5.cloned.1.call-start = ((), (), s32[]{:S(2)}) async-start(), calls=%async_computation.5 | async-start | bytes 655360 | tf_op jit(solution)/shard_map/reduce_scatter | solution.py:87
  122.2 3.8 copy-start.5
  165.4 202.9 %reduce-scatter.7.cloned.1.call-start = ((), (), s32[]{:S(2)}) async-start(), calls=%async_computation.6 | async-start | bytes 1179648 | tf_op jit(solution)/shard_map/reduce_scatter | solution.py:90
  166.6 354.9 %all-gather.5.cloned.1.call-start = ((), (), s32[]{:S(2)}) async-start(), calls=%async_computation.7 | async-start | bytes 2162688 | tf_op jit(solution)/shard_map/all_gather | solution.py:61
  411.5 1.4 copy-start.2
  466.5 237.1 %reduce-scatter.9.cloned.1.call-start = ((), (), s32[]{:S(2)}) async-start(), calls=%async_computation.8 | async-start | bytes 655360 | tf_op jit(solution)/shard_map/reduce_scatter | solution.py:87
  566.9 2.2 copy-start.3
  566.9 302.3 %copy-start.4 = (f32[1,64,64]{1,2,0:T(8,128)S(1)}, f32[1,64,64]{1,2,0:T(8,128)}, u32[]{:S(2)}) copy-start(f32[1,64,64]{1,2,0:T(8,128)} %get-tuple-element.245) | copy-start | bytes 49156
  566.9 303.1 %copy-start.1 = (f32[512,64]{0,1:T(8,128)S(1)}, f32[512,64]{0,1:T(8,128)}, u32[]{:S(2)}) copy-start(f32[512,64]{0,1:T(8,128)} %param.18) | copy-start | bytes 393220
  567.9 202.8 %reduce-scatter.11.cloned.1.call-start = ((), (), s32[]{:S(2)}) async-start(), calls=%async_computation.9 | async-start | bytes 1179648 | tf_op jit(solution)/shard_map/reduce_scatter | solution.py:90
Sparse Core Ops, SparseCore 0:
  64.0 54.8 all-gather.2
  165.6 135.4 reduce-scatter.4
  304.9 63.4 reduce-scatter.6
  466.6 54.8 all-gather.4
  568.0 135.4 reduce-scatter.8
  707.2 63.5 reduce-scatter.10
where the time goes:
time: 891 us; the launch traced here: 877 us
  waiting for transfers between devices  513 us (58%)
  blocking collectives  202 us (23%)
  other arithmetic  65.3 us (7%)
  matrix products  47.9 us (5%)
  local copies, waits for them, and re-layouts  32.7 us (4%)
  between operations  15.7 us (2%)
    reduce_scatter x2, waiting for transfers between devices, per_device(): lax.psum_scatter(part_rows.reshape(-1, vec_width), 'col', scatter_dimensi...  269 us
    reduce_scatter x2, waiting for transfers between devices, per_device(): lax.psum_scatter(part_cols.reshape(-1, vec_width), 'row', scatter_dimensi...  134 us
    all_gather x2, waiting for transfers between devices, redistribute(): gathered = lax.all_gather(packed, ('row', 'col'), axis=0, tiled=True)  109 us
    psum x2, blocking collectives, per_device(): lax.psum((jnp.dot(current.T, applied, precision=high), jnp.dot(previous.T...  81.4 us
    psum x2, blocking collectives, per_device(): lax.psum(jnp.dot(residual.T, residual, precision=high), ('row', 'col'))  78.7 us
    psum x1, blocking collectives, per_device(): lax.psum(jnp.dot(start_block.T, start_block, precision=high), ('row', 'co...  42.2 us
    scatter-add x2, other arithmetic, one_turn(): jax.ops.segment_sum(backward * live_mask[:, None, None], col_index, num_s...  27 us
    another operation x9, other arithmetic, orthonormal(): lower = jnp.linalg.cholesky(gram_now)  19.6 us
  transfers between devices with their start and end apart: 6, of which 6 were waited for; matrix products, arithmetic and copies ran while one was open for 0% of the time, Pallas kernels for 0%

commit v1 on v0

v1 whole, which is shorter than its diff:
```python
import functools

import jax
import jax.numpy as jnp
from jax import lax
from jax.experimental import pallas as pl
from jax.experimental.pallas import tpu as pltpu
from jax.sharding import PartitionSpec as P

ITERS = 2
MESH = pl.DeviceIdType.MESH
HIGH = lax.Precision.HIGHEST
NT = (((1,), (1,)), ((), ()))


def factor(gram2, width):
    row_id = lax.broadcasted_iota(jnp.int32, gram2.shape, 0)
    lane_id = lax.broadcasted_iota(jnp.int32, gram2.shape, 1)
    eye = jnp.where(lane_id - width == row_id, 1.0, 0.0)
    start = jnp.where(lane_id < width, gram2, eye)

    def step(k, now):
        row = jnp.sum(jnp.where(row_id == k, now, 0.0), axis=0, keepdims=True)
        column = jnp.sum(jnp.where(lane_id == k, now, 0.0), axis=1, keepdims=True)
        pivot = jnp.sum(jnp.where(row_id[:, :1] == k, column, 0.0), axis=0, keepdims=True)
        scale = jnp.where(row_id[:, :1] > k, column / pivot, 0.0)
        return now - scale * row

    done = lax.fori_loop(0, width, step, start)
    pivots = jnp.sum(jnp.where(lane_id == row_id, done, 0.0), axis=1, keepdims=True)
    done = done * (1.0 / jnp.sqrt(pivots))
    return jnp.where((lane_id >= width) | (lane_id >= row_id), done, 0.0)


def kernel(
    n_row, n_col, piece_blocks, total_rows,
    table_ref, blocks_hbm, start_ref,
    basis_ref, diag_ref, upper_ref,
    blocks_v, panels, row_x, col_x, row_out, col_out, row_in, col_in, row_own, col_own,
    ar_src, ar_one, ar_two, ar_three,
    load_sem, s_rx, r_rx, s_cx, r_cx, s_ro, r_ro, s_co, r_co, s_a1, r_a1, s_a2, r_a2, s_a3, r_a3,
):
    r = lax.axis_index("row")
    c = lax.axis_index("col")
    slots = blocks_hbm.shape[0]
    bs = blocks_hbm.shape[1]
    width, rows_dev = start_ref.shape
    col_blocks = n_row * piece_blocks

    load = pltpu.make_async_copy(blocks_hbm, blocks_v.at[pl.ds(0, slots)], load_sem)
    load.start()
    blocks_v[slots] = jnp.zeros((bs, bs), jnp.bfloat16)

    barrier = pltpu.get_barrier_semaphore()
    for axis, n, me in (("row", n_row, r), ("col", n_col, c)):

        def greet(k, carry, axis=axis, n=n, me=me):
            pl.semaphore_signal(
                barrier, inc=1, device_id={axis: lax.rem(me + k, n)}, device_id_type=MESH
            )
            return carry

        lax.fori_loop(1, n, greet, 0)
    pl.semaphore_wait(barrier, n_row + n_col - 2)

    def peers(axis, action):
        n, me = (n_row, r) if axis == "row" else (n_col, c)

        def body(k, carry):
            action(lax.rem(me + k, n))
            return carry

        lax.fori_loop(1, n, body, 0)

    def copy(axis, peer, src, dst, send, recv):
        return pltpu.make_async_remote_copy(
            src_ref=src, dst_ref=dst, send_sem=send, recv_sem=recv,
            device_id={axis: peer}, device_id_type=MESH,
        )

    def exchange(axis, slot, src_of, into, send, recv):
        me = r if axis == "row" else c

        def go(p):
            copy(axis, p, src_of(p), into.at[slot, me], send.at[slot, p], recv.at[slot, me]).start()

        peers(axis, go)

    def arrived(axis, slot, p, src, into, send, recv):
        copy(axis, p, src, into.at[slot, p], send.at[slot, p], recv.at[slot, p]).wait_recv()

    def sent(axis, slot, src_of, into, send, recv):
        peers(
            axis,
            lambda p: copy(
                axis, p, src_of(p), into.at[slot, p], send.at[slot, p], recv.at[slot, p]
            ).wait_send(),
        )

    def settle(axis, slot, src_of, into, send, recv):
        peers(axis, lambda p: arrived(axis, slot, p, src_of(p), into, send, recv))
        sent(axis, slot, src_of, into, send, recv)

    def add_up(into, slot, n):
        return functools.reduce(jnp.add, [into[slot, i] for i in range(n)])

    def all_reduce(slot, value):
        ar_src[slot] = value.reshape(ar_src.shape[1:])
        src = lambda p: ar_src.at[slot, p]
        exchange("col", slot, src, ar_one, s_a1, r_a1)
        ar_one[slot, c] = ar_src[slot, c]
        settle("col", slot, src, ar_one, s_a1, r_a1)
        ar_two[slot, r] = add_up(ar_one, slot, n_col)
        src = lambda p: ar_two.at[slot, r]
        exchange("row", slot, src, ar_two, s_a2, r_a2)
        settle("row", slot, src, ar_two, s_a2, r_a2)
        ar_three[slot, c] = add_up(ar_two, slot, n_row)
        src = lambda p: ar_three.at[slot, c]
        exchange("col", slot, src, ar_three, s_a3, r_a3)
        settle("col", slot, src, ar_three, s_a3, r_a3)
        return ar_three[slot].reshape(width, 2 * width)

    def gram_of(panel):
        return lax.dot_general(
            panel, jnp.concatenate([panel, panel], axis=0), NT,
            precision=HIGH, preferred_element_type=jnp.float32,
        )

    def solved(rows, panel):
        both = jnp.concatenate([jnp.zeros_like(panel), panel], axis=0)
        return jnp.dot(rows, both, precision=HIGH, preferred_element_type=jnp.float32)

    first = start_ref[...]
    rows = factor(all_reduce(0, gram_of(first)) / total_rows, width)
    panels[0] = jnp.zeros_like(first)
    panels[1] = solved(rows, first)
    load.wait()

    def block(a, b):
        return blocks_v[table_ref[a * col_blocks + b]]

    def tile(a, rows_of, b, cols_of):
        return jnp.concatenate(
            [
                jnp.concatenate([block(a + i, b + j) for j in range(cols_of)], axis=1)
                for i in range(rows_of)
            ],
            axis=0,
        )

    half = piece_blocks // 2

    def iterate(it, carry):
        current = panels[it + 1]
        packed = current.astype(jnp.bfloat16)
        row_x[it, c] = packed
        col_x[it, r] = packed
        src_rx = lambda p: row_x.at[it, c]
        src_cx = lambda p: col_x.at[it, r]
        exchange("col", it, src_rx, row_x, s_rx, r_rx)
        exchange("row", it, src_cx, col_x, s_cx, r_cx)
        settle("col", it, src_rx, row_x, s_rx, r_rx)

        def backward(k, carry):
            p = lax.rem(r + k, n_row)
            for h in range(2):
                total = jnp.zeros((width, half * bs), jnp.float32)
                for q in range(n_col):
                    total += jnp.dot(
                        row_x[it, q],
                        tile(q * piece_blocks, piece_blocks, p * piece_blocks + h * half, half),
                        preferred_element_type=jnp.float32,
                    )
                at = pl.ds(h * half * bs, half * bs)
                col_own[:, at] = total
                col_out[p, :, at] = total.astype(jnp.bfloat16)

            @pl.when(k < n_row)
            def _():
                copy(
                    "row", p, col_out.at[p], col_in.at[it, r], s_co.at[it, p], r_co.at[it, r]
                ).start()

            return carry

        lax.fori_loop(1, n_row + 1, backward, 0)
        settle("row", it, src_cx, col_x, s_cx, r_cx)

        def forward(k, carry):
            q = lax.rem(c + k, n_col)

            def add_piece(p, totals):
                piece = col_x[it, p]
                return tuple(
                    totals[h]
                    + lax.dot_general(
                        piece,
                        tile(q * piece_blocks + h * half, half, p * piece_blocks, piece_blocks),
                        NT,
                        preferred_element_type=jnp.float32,
                    )
                    for h in range(2)
                )

            zero = jnp.zeros((width, half * bs), jnp.float32)
            totals = lax.fori_loop(0, n_row, add_piece, (zero, zero))
            for h in range(2):
                at = pl.ds(h * half * bs, half * bs)
                row_own[:, at] = totals[h]
                row_out[q, :, at] = totals[h].astype(jnp.bfloat16)

            @pl.when(k < n_col)
            def _():
                copy(
                    "col", q, row_out.at[q], row_in.at[it, c], s_ro.at[it, q], r_ro.at[it, c]
                ).start()

            return carry

        lax.fori_loop(1, n_col + 1, forward, 0)
        col_own[...] += current + row_own[...]

        def take_col(p):
            arrived("row", it, p, col_out.at[p], col_in, s_co, r_co)
            col_own[...] += col_in[it, p].astype(jnp.float32)

        def take_row(p):
            arrived("col", it, p, row_out.at[p], row_in, s_ro, r_ro)
            col_own[...] += row_in[it, p].astype(jnp.float32)

        peers("row", take_col)
        peers("col", take_row)
        sent("row", it, lambda p: col_out.at[p], col_in, s_co, r_co)
        sent("col", it, lambda p: row_out.at[p], row_in, s_ro, r_ro)

        applied = col_own[...]
        pair = jnp.concatenate([current, panels[it]], axis=0)
        along = lax.dot_general(
            applied, pair, NT, precision=HIGH, preferred_element_type=jnp.float32
        )
        along = all_reduce(1 + 2 * it, along) / total_rows
        diag_ref[it] = along
        residual = applied - jnp.dot(
            along, pair, precision=HIGH, preferred_element_type=jnp.float32
        )
        rows = factor(all_reduce(2 + 2 * it, gram_of(residual)) / total_rows, width)
        upper_ref[it] = rows
        panels[it + 2] = solved(rows, residual)
        return carry

    lax.fori_loop(0, ITERS, iterate, 0)
    basis_ref[...] = panels[ITERS + 1]


def per_device(blocks, coords, counts, start_block):
    rows_dev, width = start_block.shape
    slots, bs, _ = blocks.shape
    n_row = lax.axis_size("row")
    n_col = lax.axis_size("col")
    piece_blocks = rows_dev // bs
    row_blocks = n_col * piece_blocks
    col_blocks = n_row * piece_blocks
    slot_ids = jnp.arange(slots, dtype=jnp.int32)
    place = coords[:, 0] * col_blocks + coords[:, 1]
    places = jnp.arange(row_blocks * col_blocks, dtype=jnp.int32)
    hit = (places[:, None] == place[None, :]) & (slot_ids < counts[0])[None, :]
    table = jnp.min(jnp.where(hit, slot_ids[None, :], slots), axis=1)

    quarter = width // n_col
    sums = 1 + 2 * ITERS
    dma = pltpu.SemaphoreType.DMA
    bf16, f32 = jnp.bfloat16, jnp.float32
    vmem = pl.BlockSpec(memory_space=pltpu.VMEM)
    basis, diag, upper = pl.pallas_call(
        functools.partial(
            kernel, n_row, n_col, piece_blocks, float(rows_dev * n_row * n_col)
        ),
        out_shape=(
            jax.ShapeDtypeStruct((width, rows_dev), f32),
            jax.ShapeDtypeStruct((ITERS, width, 2 * width), f32),
            jax.ShapeDtypeStruct((ITERS, width, 2 * width), f32),
        ),
        in_specs=[
            pl.BlockSpec(memory_space=pltpu.SMEM),
            pl.BlockSpec(memory_space=pl.ANY),
            vmem,
        ],
        out_specs=(vmem, vmem, vmem),
        scratch_shapes=[
            pltpu.VMEM((slots + 1, bs, bs), bf16),
            pltpu.VMEM((ITERS + 2, width, rows_dev), f32),
            pltpu.VMEM((ITERS, n_col, width, rows_dev), bf16),
            pltpu.VMEM((ITERS, n_row, width, rows_dev), bf16),
            pltpu.VMEM((n_col, width, rows_dev), bf16),
            pltpu.VMEM((n_row, width, rows_dev), bf16),
            pltpu.VMEM((ITERS, n_col, width, rows_dev), bf16),
            pltpu.VMEM((ITERS, n_row, width, rows_dev), bf16),
            pltpu.VMEM((width, rows_dev), f32),
            pltpu.VMEM((width, rows_dev), f32),
            pltpu.VMEM((sums, n_col, quarter, 2 * width), f32),
            pltpu.VMEM((sums, n_col, quarter, 2 * width), f32),
            pltpu.VMEM((sums, n_row, quarter, 2 * width), f32),
            pltpu.VMEM((sums, n_col, quarter, 2 * width), f32),
            dma,
            dma((ITERS, n_col)), dma((ITERS, n_col)),
            dma((ITERS, n_row)), dma((ITERS, n_row)),
            dma((ITERS, n_col)), dma((ITERS, n_col)),
            dma((ITERS, n_row)), dma((ITERS, n_row)),
            dma((sums, n_col)), dma((sums, n_col)),
            dma((sums, n_row)), dma((sums, n_row)),
            dma((sums, n_col)), dma((sums, n_col)),
        ],
        compiler_params=pltpu.CompilerParams(
            collective_id=0, has_side_effects=True, vmem_limit_bytes=48 * 1024 * 1024
        ),
    )(table, blocks, start_block.T)
    return (
        basis.T,
        jnp.swapaxes(diag[:, :, :width], 1, 2),
        upper[:, :, :width],
    )


def solution(mesh):
    return jax.shard_map(
        per_device,
        mesh=mesh,
        in_specs=(
            P(("row", "col"), None, None),
            P(("row", "col"), None),
            P(("row", "col")),
            P(("row", "col"), None),
        ),
        out_specs=(P(("row", "col"), None), P(), P()),
        check_vma=False,
    )
```

time: 891 us -> 143 us (0.16); the launches traced: 877 us -> 143 us
  waiting for transfers between devices: 513 us -> 0 us
  blocking collectives: 202 us -> 0 us
  Pallas kernels: 0 us -> 137 us
  other arithmetic: 65.3 us -> 1.09 us
  matrix products: 47.9 us -> 0 us
  local copies, waits for them, and re-layouts: 32.7 us -> 2.9 us
  between operations: 15.7 us -> 1.31 us
    reduce_scatter x4 -> x0, waiting for transfers between devices: 403 us -> none  [the longest x2 269 us: per_device(): lax.psum_scatter(part_rows.reshape(-1, vec_width), 'col', scatter_dimensi...]
    psum x5 -> x0, blocking collectives: 202 us -> none  [the longest x2 81.4 us: per_device(): lax.psum((jnp.dot(current.T, applied, precision=high), jnp.dot(previous.T...]
    pallas_call x0 -> x1, Pallas kernels: none -> 137 us  [per_device(): pl.pallas_call(functools.partial(kernel, n_row, n_col, piece_blocks, floa...]
    all_gather x2 -> x0, waiting for transfers between devices: 109 us -> none  [redistribute(): gathered = lax.all_gather(packed, ('row', 'col'), axis=0, tiled=True)]
    dot_general x19 -> x0, matrix products: 47.2 us -> none  [the longest x2 14.1 us: one_turn(): jnp.einsum('gij,gik->gjk', slab, row_rows, preferred_element_type=jnp.flo...]
    another operation x20 -> x0, other arithmetic: 36.9 us -> none  [the longest x9 19.6 us: orthonormal(): lower = jnp.linalg.cholesky(gram_now)]
    scatter-add x2 -> x0, other arithmetic: 27 us -> none  [one_turn(): jax.ops.segment_sum(backward * live_mask[:, None, None], col_index, num_s...]
    gather x4 -> x0, local copies, waits for them, and re-layouts: 12 us -> none  [the longest x2 6.02 us: one_turn(): col_rows = jnp.take(col_x, col_index, axis=0)]
  transfers between devices with their start and end apart: 6 -> 0, of which waited for: 6 -> 0; matrix products, arithmetic and copies ran while one was open for 0% -> 0% of each run, Pallas kernels for 0% -> 0%
where the time goes in v1:
time: 143 us
  Pallas kernels  137 us (96%)
  local copies, waits for them, and re-layouts  2.9 us (2%)
    pallas_call x1, Pallas kernels, per_device(): pl.pallas_call(functools.partial(kernel, n_row, n_col, piece_blocks, floa...  137 us
    unnamed x5, local copies, waits for them, and re-layouts  2.89 us

profile of v1, /device:TPU:0, one launch (start us, length us, event | category | flops | bytes accessed | tf_op | source)
XLA Modules:
  0.0 142.5 jit_solution(3928169180121433743)
XLA Ops:
  1.3 0.8 slice_add_fusion
  2.1 0.3 select_reduce_fusion.table_ref
  2.4 0.0 copy-start
  2.4 0.9 copy-done
  3.3 137.2 %shard_map.67 = (f32[64,512]{1,0:T(8,128)S(1)}, f32[2,64,128]{2,1,0:T(8,128)S(1)}, f32[2,64,128]{2,1,0:T(8,128)S(1)}) custom-call(s32[512]{0:T(512)S(1)} %select_reduce_fusion.table_ref, bf16[512,128,128]{2,1,0:T(8,128)(2,1)} %blocks_hbm.1, f32[64,512]{1,0:T(8,128)S(1)} %bitcast.8), custom_call_target="tpu_custom_call" | custom-call | tf_op jit(solution)/shard_map/pallas_call | solution.py:274
  140.5 0.7 copy.8
  141.2 0.7 copy.12
  141.9 0.6 copy.13
  (2 shorter events, 0.0 us)
Async XLA Ops:
  2.4 0.9 copy-start

commit v2 on v1

--- a/solution.py
+++ b/solution.py
@@ -11,25 +11,35 @@
 MESH = pl.DeviceIdType.MESH
 HIGH = lax.Precision.HIGHEST
 NT = (((1,), (1,)), ((), ()))
+GROUP = 4
 
 
 def factor(gram2, width):
     row_id = lax.broadcasted_iota(jnp.int32, gram2.shape, 0)
     lane_id = lax.broadcasted_iota(jnp.int32, gram2.shape, 1)
     eye = jnp.where(lane_id - width == row_id, 1.0, 0.0)
-    start = jnp.where(lane_id < width, gram2, eye)
-
-    def step(k, now):
-        row = jnp.sum(jnp.where(row_id == k, now, 0.0), axis=0, keepdims=True)
-        column = jnp.sum(jnp.where(lane_id == k, now, 0.0), axis=1, keepdims=True)
-        pivot = jnp.sum(jnp.where(row_id[:, :1] == k, column, 0.0), axis=0, keepdims=True)
-        scale = jnp.where(row_id[:, :1] > k, column / pivot, 0.0)
-        return now - scale * row
-
-    done = lax.fori_loop(0, width, step, start)
-    pivots = jnp.sum(jnp.where(lane_id == row_id, done, 0.0), axis=1, keepdims=True)
-    done = done * (1.0 / jnp.sqrt(pivots))
-    return jnp.where((lane_id >= width) | (lane_id >= row_id), done, 0.0)
+    now = jnp.where(lane_id < width, gram2, eye)
+    for k in range(0, width, GROUP):
+        columns = [
+            jnp.broadcast_to(now[:, k + j : k + j + 1], now.shape) for j in range(GROUP)
+        ]
+        rows = [now[k + j : k + j + 1, :] for j in range(GROUP)]
+        scaled = []
+        for j in range(GROUP):
+            inverse = 1.0 / columns[j][k + j : k + j + 1, :]
+            for i in range(j + 1, GROUP):
+                ratio = columns[j][k + i : k + i + 1, :] * inverse
+                rows[i] = rows[i] - ratio * rows[j]
+                columns[i] = columns[i] - ratio * columns[j]
+            scaled.append(rows[j] * inverse)
+        update = functools.reduce(jnp.add, [columns[j] * scaled[j] for j in range(GROUP)])
+        later = jnp.where(row_id >= k + GROUP, now - update, now)
+        for j in range(GROUP):
+            later = jnp.where(row_id == k + j, rows[j], later)
+        now = later
+    pivots = jnp.sum(jnp.where(lane_id == row_id, now, 0.0), axis=1, keepdims=True)
+    now = now * (1.0 / jnp.sqrt(pivots))
+    return jnp.where((lane_id >= width) | (lane_id >= row_id), now, 0.0)
 
 
 def kernel(
@@ -78,47 +88,56 @@
             device_id={axis: peer}, device_id_type=MESH,
         )
 
-    def exchange(axis, slot, src_of, into, send, recv):
+    def exchange(axis, slot, src_of, into, send, recv, rows=slice(None)):
         me = r if axis == "row" else c
 
         def go(p):
-            copy(axis, p, src_of(p), into.at[slot, me], send.at[slot, p], recv.at[slot, me]).start()
+            copy(axis, p, src_of(p), into.at[slot, me, rows], send.at[slot, p], recv.at[slot, me]).start()
 
         peers(axis, go)
 
-    def arrived(axis, slot, p, src, into, send, recv):
-        copy(axis, p, src, into.at[slot, p], send.at[slot, p], recv.at[slot, p]).wait_recv()
-
-    def sent(axis, slot, src_of, into, send, recv):
+    def arrived(axis, slot, p, src, into, send, recv, rows=slice(None)):
+        copy(axis, p, src, into.at[slot, p, rows], send.at[slot, p], recv.at[slot, p]).wait_recv()
+
+    def sent(axis, slot, src_of, into, send, recv, rows=slice(None)):
         peers(
             axis,
             lambda p: copy(
-                axis, p, src_of(p), into.at[slot, p], send.at[slot, p], recv.at[slot, p]
+                axis, p, src_of(p), into.at[slot, p, rows], send.at[slot, p], recv.at[slot, p]
             ).wait_send(),
         )
 
-    def settle(axis, slot, src_of, into, send, recv):
-        peers(axis, lambda p: arrived(axis, slot, p, src_of(p), into, send, recv))
-        sent(axis, slot, src_of, into, send, recv)
-
-    def add_up(into, slot, n):
-        return functools.reduce(jnp.add, [into[slot, i] for i in range(n)])
+    def settle(axis, slot, src_of, into, send, recv, rows=slice(None)):
+        peers(axis, lambda p: arrived(axis, slot, p, src_of(p), into, send, recv, rows))
+        sent(axis, slot, src_of, into, send, recv, rows)
+
+    def add_up(into, slot, n, rows):
+        return functools.reduce(jnp.add, [into[slot, i, rows] for i in range(n)])
 
     def all_reduce(slot, value):
-        ar_src[slot] = value.reshape(ar_src.shape[1:])
-        src = lambda p: ar_src.at[slot, p]
-        exchange("col", slot, src, ar_one, s_a1, r_a1)
-        ar_one[slot, c] = ar_src[slot, c]
-        settle("col", slot, src, ar_one, s_a1, r_a1)
-        ar_two[slot, r] = add_up(ar_one, slot, n_col)
-        src = lambda p: ar_two.at[slot, r]
-        exchange("row", slot, src, ar_two, s_a2, r_a2)
-        settle("row", slot, src, ar_two, s_a2, r_a2)
-        ar_three[slot, c] = add_up(ar_two, slot, n_row)
-        src = lambda p: ar_three.at[slot, c]
-        exchange("col", slot, src, ar_three, s_a3, r_a3)
-        settle("col", slot, src, ar_three, s_a3, r_a3)
-        return ar_three[slot].reshape(width, 2 * width)
+        part = value.shape[0] // n_col
+        rows = pl.ds(0, part)
+        ar_src[slot, :, rows] = value.reshape(n_col, part, 2 * width)
+        src = lambda p: ar_src.at[slot, p, rows]
+        exchange("col", slot, src, ar_one, s_a1, r_a1, rows)
+        ar_one[slot, c, rows] = ar_src[slot, c, rows]
+        settle("col", slot, src, ar_one, s_a1, r_a1, rows)
+        ar_two[slot, r, rows] = add_up(ar_one, slot, n_col, rows)
+        src = lambda p: ar_two.at[slot, r, rows]
+        exchange("row", slot, src, ar_two, s_a2, r_a2, rows)
+        settle("row", slot, src, ar_two, s_a2, r_a2, rows)
+        ar_three[slot, c, rows] = add_up(ar_two, slot, n_row, rows)
+        src = lambda p: ar_three.at[slot, c, rows]
+        exchange("col", slot, src, ar_three, s_a3, r_a3, rows)
+        settle("col", slot, src, ar_three, s_a3, r_a3, rows)
+        return ar_three[slot, :, rows].reshape(value.shape)
+
+    def fold(gram2):
+        lane_id = lax.broadcasted_iota(jnp.int32, (width // 2, 2 * width), 1)
+        return jnp.where(lane_id < width, gram2[: width // 2], gram2[width // 2 :])
+
+    def unfold(folded):
+        return jnp.concatenate([folded, pltpu.roll(folded, width, 1)], axis=0)
 
     def gram_of(panel):
         return lax.dot_general(
@@ -131,7 +150,7 @@
         return jnp.dot(rows, both, precision=HIGH, preferred_element_type=jnp.float32)
 
     first = start_ref[...]
-    rows = factor(all_reduce(0, gram_of(first)) / total_rows, width)
+    rows = factor(unfold(all_reduce(0, fold(gram_of(first)))) / total_rows, width)
     panels[0] = jnp.zeros_like(first)
     panels[1] = solved(rows, first)
     load.wait()
@@ -218,7 +237,7 @@
             return carry
 
         lax.fori_loop(1, n_col + 1, forward, 0)
-        col_own[...] += current + row_own[...]
+        col_own[...] += row_own[...]
 
         def take_col(p):
             arrived("row", it, p, col_out.at[p], col_in, s_co, r_co)
@@ -238,12 +257,16 @@
         along = lax.dot_general(
             applied, pair, NT, precision=HIGH, preferred_element_type=jnp.float32
         )
-        along = all_reduce(1 + 2 * it, along) / total_rows
-        diag_ref[it] = along
+        sums = all_reduce(1 + it, jnp.concatenate([along, fold(gram_of(applied))], axis=0))
+        along = sums[:width] / total_rows
+        row_id = lax.broadcasted_iota(jnp.int32, along.shape, 0)
+        lane_id = lax.broadcasted_iota(jnp.int32, along.shape, 1)
+        diag_ref[it] = along + jnp.where(row_id == lane_id, 1.0, 0.0)
         residual = applied - jnp.dot(
             along, pair, precision=HIGH, preferred_element_type=jnp.float32
         )
-        rows = factor(all_reduce(2 + 2 * it, gram_of(residual)) / total_rows, width)
+        gram = unfold(sums[width:]) / total_rows - gram_of(along)
+        rows = factor(gram, width)
         upper_ref[it] = rows
         panels[it + 2] = solved(rows, residual)
         return carry
@@ -266,8 +289,8 @@
     hit = (places[:, None] == place[None, :]) & (slot_ids < counts[0])[None, :]
     table = jnp.min(jnp.where(hit, slot_ids[None, :], slots), axis=1)
 
-    quarter = width // n_col
-    sums = 1 + 2 * ITERS
+    quarter = (width + width // 2) // n_col
+    sums = 1 + ITERS
     dma = pltpu.SemaphoreType.DMA
     bf16, f32 = jnp.bfloat16, jnp.float32
     vmem = pl.BlockSpec(memory_space=pltpu.VMEM)

time: 143 us -> 110 us (0.77)
  Pallas kernels: 137 us -> 105 us
    pallas_call x1, Pallas kernels: 137 us -> 105 us  [per_device(): pl.pallas_call(functools.partial(kernel, n_row, n_col, piece_blocks, floa...]
where the time goes in v2:
time: 110 us
  Pallas kernels  105 us (95%)
  local copies, waits for them, and re-layouts  2.9 us (3%)
  between operations  1.31 us (1%)
    pallas_call x1, Pallas kernels, per_device(): pl.pallas_call(functools.partial(kernel, n_row, n_col, piece_blocks, floa...  105 us
    unnamed x5, local copies, waits for them, and re-layouts  2.89 us

profile of v2, /device:TPU:0, one launch (start us, length us, event | category | flops | bytes accessed | tf_op | source)
XLA Modules:
  0.0 109.9 jit_solution(7639815245156188485)
XLA Ops:
  1.3 0.8 slice_add_fusion
  2.1 0.3 select_reduce_fusion.table_ref
  2.4 0.0 copy-start
  2.4 0.9 copy-done
  3.3 104.6 %shard_map.67 = (f32[64,512]{1,0:T(8,128)S(1)}, f32[2,64,128]{2,1,0:T(8,128)S(1)}, f32[2,64,128]{2,1,0:T(8,128)S(1)}) custom-call(s32[512]{0:T(512)S(1)} %select_reduce_fusion.table_ref, bf16[512,128,128]{2,1,0:T(8,128)(2,1)} %blocks_hbm.1, f32[64,512]{1,0:T(8,128)S(1)} %bitcast.8), custom_call_target="tpu_custom_call" | custom-call | tf_op jit(solution)/shard_map/pallas_call | solution.py:297
  107.9 0.7 copy.8
  108.6 0.7 copy.12
  109.3 0.6 copy.13
  (2 shorter events, 0.0 us)
Async XLA Ops:
  2.4 0.9 copy-start

commit v3 on v2

--- a/solution.py
+++ b/solution.py
@@ -11,7 +11,7 @@
 MESH = pl.DeviceIdType.MESH
 HIGH = lax.Precision.HIGHEST
 NT = (((1,), (1,)), ((), ()))
-GROUP = 4
+GROUP = 8
 
 
 def factor(gram2, width):
@@ -82,6 +82,18 @@
 
         lax.fori_loop(1, n, body, 0)
 
+    def twin(p):
+        return p + 1 - 2 * lax.rem(p, 2)
+
+    pairs = n_row // 2
+
+    def alike(action):
+        def body(k, carry):
+            action(lax.rem(r + 2 * k, n_row))
+            return carry
+
+        lax.fori_loop(1, pairs, body, 0)
+
     def copy(axis, peer, src, dst, send, recv):
         return pltpu.make_async_remote_copy(
             src_ref=src, dst_ref=dst, send_sem=send, recv_sem=recv,
@@ -175,13 +187,34 @@
         row_x[it, c] = packed
         col_x[it, r] = packed
         src_rx = lambda p: row_x.at[it, c]
-        src_cx = lambda p: col_x.at[it, r]
+
+        def give(p, piece):
+            at = jnp.where(p == twin(r), twin(piece), p)
+            return copy(
+                "row", p, col_x.at[it, piece], col_x.at[it, piece],
+                s_cx.at[it, at], r_cx.at[it, piece],
+            )
+
         exchange("col", it, src_rx, row_x, s_rx, r_rx)
-        exchange("row", it, src_cx, col_x, s_cx, r_cx)
+        alike(lambda p: give(p, r).start())
+        give(twin(r), r).start()
         settle("col", it, src_rx, row_x, s_rx, r_rx)
 
+        def to_twin(p):
+            at = twin(p)
+            return copy(
+                "row", twin(r), col_out.at[p], col_in.at[it, at], s_co.at[it, p], r_co.at[it, at]
+            )
+
         def backward(k, carry):
-            p = lax.rem(r + k, n_row)
+            @pl.when((lax.rem(k, 2) == 1) & (k > 1))
+            def _():
+                piece = lax.rem(r + n_row + 1 - k, n_row)
+                give(twin(r), piece).wait_recv()
+                give(twin(r), piece).start()
+
+            base = jnp.where(k < pairs, twin(r), r)
+            p = lax.rem(base + 2 * (lax.rem(k, pairs) + 1), n_row)
             for h in range(2):
                 total = jnp.zeros((width, half * bs), jnp.float32)
                 for q in range(n_col):
@@ -192,18 +225,35 @@
                     )
                 at = pl.ds(h * half * bs, half * bs)
                 col_own[:, at] = total
-                col_out[p, :, at] = total.astype(jnp.bfloat16)
-
-            @pl.when(k < n_row)
+
+            @pl.when(k < pairs)
             def _():
+                col_out[p] = col_own[...].astype(jnp.bfloat16)
+                to_twin(p).start()
+
+            @pl.when(k >= pairs)
+            def _():
+                to_twin(p).wait_recv()
+                col_own[...] += col_in[it, twin(p)].astype(jnp.float32)
+
+            @pl.when((k >= pairs) & (k < n_row - 1))
+            def _():
+                col_out[p] = col_own[...].astype(jnp.bfloat16)
                 copy(
                     "row", p, col_out.at[p], col_in.at[it, r], s_co.at[it, p], r_co.at[it, r]
                 ).start()
 
             return carry
 
-        lax.fori_loop(1, n_row + 1, backward, 0)
-        settle("row", it, src_cx, col_x, s_cx, r_cx)
+        lax.fori_loop(0, n_row, backward, 0)
+
+        def from_twin(k, carry):
+            piece = lax.rem(twin(r) + 2 * k, n_row)
+            give(twin(r), piece).wait_recv()
+            return carry
+
+        lax.fori_loop(0, pairs, from_twin, 0)
+        peers("row", lambda p: give(p, r).wait_send())
 
         def forward(k, carry):
             q = lax.rem(c + k, n_col)
@@ -247,7 +297,7 @@
             arrived("col", it, p, row_out.at[p], row_in, s_ro, r_ro)
             col_own[...] += row_in[it, p].astype(jnp.float32)
 
-        peers("row", take_col)
+        alike(take_col)
         peers("col", take_row)
         sent("row", it, lambda p: col_out.at[p], col_in, s_co, r_co)
         sent("col", it, lambda p: row_out.at[p], row_in, s_ro, r_ro)

time: 110 us -> 103 us (0.936)
  Pallas kernels: 105 us -> 97.8 us
    pallas_call x1, Pallas kernels: 105 us -> 97.8 us  [per_device(): pl.pallas_call(functools.partial(kernel, n_row, n_col, piece_blocks, floa...]
where the time goes in v3:
time: 103 us
  Pallas kernels  97.8 us (95%)
  local copies, waits for them, and re-layouts  2.9 us (3%)
  between operations  1.31 us (1%)
  other arithmetic  1.09 us (1%)
    pallas_call x1, Pallas kernels, per_device(): pl.pallas_call(functools.partial(kernel, n_row, n_col, piece_blocks, floa...  97.8 us
    unnamed x5, local copies, waits for them, and re-layouts  2.89 us

profile of v3, /device:TPU:0, one launch (start us, length us, event | category | flops | bytes accessed | tf_op | source)
XLA Modules:
  0.0 103.1 jit_solution(2061141029750933264)
XLA Ops:
  1.3 0.8 slice_add_fusion
  2.1 0.3 select_reduce_fusion.table_ref
  2.4 0.0 copy-start
  2.4 0.9 copy-done
  3.3 97.8 %shard_map.67 = (f32[64,512]{1,0:T(8,128)S(1)}, f32[2,64,128]{2,1,0:T(8,128)S(1)}, f32[2,64,128]{2,1,0:T(8,128)S(1)}) custom-call(s32[512]{0:T(512)S(1)} %select_reduce_fusion.table_ref, bf16[512,128,128]{2,1,0:T(8,128)(2,1)} %blocks_hbm.1, f32[64,512]{1,0:T(8,128)S(1)} %bitcast.8), custom_call_target="tpu_custom_call" | custom-call | tf_op jit(solution)/shard_map/pallas_call | solution.py:347
  101.1 0.7 copy.8
  101.8 0.7 copy.12
  102.4 0.6 copy.13
  (2 shorter events, 0.0 us)
Async XLA Ops:
  2.4 0.9 copy-start
